TPU v7x, 32 devices: a whole 2x2x4 slice. The times are simulated.
32 devices in a mesh: space: 4 (over y, core), tm: 8 (over z, x).
Axes of the slice: x: 2, y: 2, z: 4, core: 2. Of those that a mesh axis runs over, the one named last changes fastest.
Arguments:
- space_factor: bfloat16 [64, 16384], P('tm', 'space'), may hold values from -2.5 to 2.5
- time_factor: bfloat16 [64, 2048], P('space', 'tm'), may hold values from -2.5 to 2.5
- initial_state: float32 [16384], P('space'), may hold values from -6 to 6
- link: int32 [16384], P('space'), may hold values from 1 to 4
- conductivity: float32 [16384], P('space'), may hold values from 0.2 to 2
- mass: float32 [16384], P('space'), may hold values from 0.5 to 2
- reaction: float32 [16384], P('space'), may hold values from 0.05 to 0.4
- source: bfloat16 [16384, 2048], P('space', 'tm'), may hold values from -6 to 6
Outputs:
- grad_space: float32 [64, 16384], P('tm', 'space')
- grad_time: float32 [64, 2048], P('space', 'tm')
Inputs may be any that keep to these rules, and one draw needn't show every extreme that they name: Element i joins node i and node i + link[i]; where that node lies past the last node, the element ties node i to a zero value.
All inputs are finite; a program needn't handle non-finite values.
Results may differ from a plain program's by a relative error of at most 0.00055.
Values may be sent and summed in bfloat16 or wider, within the bound.
A program may use at most 64 MiB of HBM per device.

v0:
```python
import math

import jax
import jax.numpy as jnp
from jax import lax
from jax.sharding import PartitionSpec as P

W = 4


def from_behind(array, axis, by):
    length = lax.axis_size(axis)
    pairs = [(i, i + by) for i in range(length) if 0 <= i + by < length]
    return lax.ppermute(array, axis, pairs)


def padded_2(array, sides, width):
    for axis, dim in sides:
        size, length = (lax.axis_size(axis), array.shape[dim])
        up = [(i, (i + 1) % size) for i in range(size - 1)]
        down = [(j, i) for i, j in up]
        last = lax.slice_in_dim(array, length - width, length, axis=dim)
        initial = lax.slice_in_dim(array, 0, width, axis=dim)
        before = lax.ppermute(last, axis, up)
        after = lax.ppermute(initial, axis, down)
        array = jnp.concatenate([before, array, after], axis=dim)
    return array


def diffuse(padded, rates_padded, count):
    total = None
    for offset in range(1, W + 1):
        own_rate = rates_padded[offset - 1, W : W + count][:, None]
        came_rate = rates_padded[offset - 1, W - offset : W - offset + count][:, None]
        centre = padded[W : W + count]
        term = own_rate * (centre - padded[W + offset : W + offset + count]) - came_rate * (
            padded[W - offset : W - offset + count] - centre
        )
        total = term if total is None else total + term
    return total


def contract(left, right):
    return lax.dot_general(
        left, right, (((0,), (0,)), ((), ())), preferred_element_type=jnp.float32
    )


def body(space_factor, time_factor, initial_state, link, conductivity, mass, reaction, source):
    node_count = space_factor.shape[1]
    step_count = time_factor.shape[1]
    time_full = lax.all_gather(time_factor, "space", axis=0, tiled=True)
    earlier_row = None
    earlier_row = from_behind(time_full[:, -1], "tm", 1)
    space_full = None
    carried = None
    space_full = lax.all_gather(space_factor, "tm", axis=0, tiled=True)
    state = contract(space_full, time_full)
    carried = contract(space_full, earlier_row)
    leading = lax.axis_index("tm") == 0
    prior_col = jnp.where(leading, initial_state, carried)
    earlier = jnp.concatenate([prior_col[:, None], state[:, :-1]], axis=1)
    offsets = jnp.arange(1, W + 1, dtype=jnp.int32)[:, None]
    rates = jnp.where(link[None, :] == offsets, conductivity[None, :], 0.0)
    below_rates = from_behind(rates[:, node_count - W :], "space", 1)
    rates_padded = jnp.concatenate([below_rates, rates], axis=1)
    padded = padded_2(state, (("space", 0),), W)
    mass_col = mass[:, None]
    react_col = reaction[:, None]
    residual = (
        mass_col * (state - earlier)
        + diffuse(padded, rates_padded, node_count)
        + react_col * state * state * state
        - source.astype(jnp.float32)
    )
    following = from_behind(residual[:, 0], "tm", -1)
    later = jnp.concatenate([residual[:, 1:], following[:, None]], axis=1)
    padded_residual = padded_2(residual, (("space", 0),), W)
    descent = (
        mass_col * (residual - later)
        + diffuse(padded_residual, rates_padded, node_count)
        + 3.0 * react_col * state * state * residual
    )
    descent_b = descent.astype(jnp.bfloat16)
    steps_all = step_count * lax.axis_size("tm")
    nodes_all = node_count * lax.axis_size("space")
    picked = time_full
    grad_space = lax.psum_scatter(
        lax.dot_general(
            picked, descent_b, (((1,), (1,)), ((), ())), preferred_element_type=jnp.float32
        ),
        "tm",
        scatter_dimension=0,
        tiled=True,
    ) / math.sqrt(steps_all)
    picked = space_full
    node_sums = lax.psum_scatter(
        jnp.dot(picked, descent_b, preferred_element_type=jnp.float32),
        "space",
        scatter_dimension=0,
        tiled=True,
    )
    grad_time = node_sums / math.sqrt(nodes_all)
    return (grad_space, grad_time)


def solution(mesh):
    in_specs = (
        P("tm", "space"),
        P("space", "tm"),
        P("space"),
        P("space"),
        P("space"),
        P("space"),
        P("space"),
        P("space", "tm"),
    )
    out_specs = (P("tm", "space"), P("space", "tm"))
    return jax.shard_map(body, mesh=mesh, in_specs=in_specs, out_specs=out_specs, check_vma=False)
```

profile of v0, /device:TPU:0, one launch (start us, length us, event | category | flops | bytes accessed | tf_op | source)
XLA Modules:
  0.0 212.9 jit_solution(5059418927405164059)
XLA Ops:
  7.2 0.0 copy-start.4
  7.2 0.0 reduce-scatter.5.cloned.1.call-start
  7.2 6.4 %all_gather.7 = bf16[64,256]{1,0:T(8,128)(2,1)S(1)} all-gather(bf16[16,256]{1,0:T(8,128)(2,1)} %param.9), channel_id=1, replica_groups=mesh['space'=4,'tm'=8] {'space'}, dimensions={0}, use_global_device_ids=true | all-gather | bytes 40960 | tf_op jit(solution)/shard_map/all_gather | solution.py:52
  13.6 0.2 slice_reduce_fusion.1
  13.8 3.8 %collective-permute-start = (bf16[64]{0:T(256)(128)(2,1)S(1)}, bf16[64]{0:T(256)(128)(2,1)S(1)}, u32[]{:S(2)}, u32[]{:S(2)}) collective-permute-start(bf16[64]{0:T(256)(128)(2,1)S(1)} %slice_reduce_fusion.1), channel_id=1, source_target_pairs={{0,1},{1,2},{2,3},{3,4},{4,5},{5,6},{6,7},{8,9},{9,10},{10,11},{11... | collective-permute-start | bytes 392 | tf_op jit(solution)/shard_map/ppermute | solution.py:14
  17.7 0.8 compare_select_fusion
  18.5 0.0 copy-start.2
  18.5 0.0 copy-start.3
  18.5 0.1 slice.162
  18.6 1.9 collective-permute-start.2
  20.5 32.1 %all_gather.6 = bf16[64,4096]{1,0:T(8,128)(2,1)S(1)} all-gather(bf16[8,4096]{1,0:T(8,128)(2,1)} %param.8), channel_id=1, replica_groups=mesh['space'=4,'tm'=8] {'tm'}, dimensions={0}, use_global_device_ids=true | all-gather | bytes 589824 | tf_op jit(solution)/shard_map/all_gather | solution.py:57
  52.6 0.7 fusion.71
  53.4 0.0 copy-start
  53.4 1.9 copy-done
  55.3 1.3 collective-permute-start.1
  56.6 3.0 %collective-permute-start.3 = (f32[4,256]{1,0:T(4,128)S(1)}, f32[4,256]{1,0:T(4,128)S(1)}, u32[]{:S(2)}, u32[]{:S(2)}) collective-permute-start(f32[4,256]{1,0:T(4,128)S(1)} %get-tuple-element.5), channel_id=1, source_target_pairs={{0,8},{8,16},{16,24},{1,9},{9,17},{17,25},{2,10},{10,18},{18,26},{... | collective-permute-start | bytes 12296 | tf_op jit(solution)/shard_map/ppermute | solution.py:24
  59.7 0.0 collective-permute-done.2
  59.7 0.2 pad_maximum_fusion.7
  59.9 0.0 collective-permute-done
  59.9 0.2 fusion.67
  60.1 0.0 copy-done.4
  60.1 0.6 copy.10
  60.7 0.0 collective-permute-done.1
  60.7 0.0 collective-permute-done.3
  60.8 0.0 copy-done.2
  60.8 0.0 copy-done.3
  60.8 22.1 %fusion.1 = f32[4096,256]{1,0:T(8,128)S(1)} fusion(f32[4096,256]{1,0:T(8,128)} %copy-done, f32[4,256]{1,0:T(4,128)S(1)} %collective-permute-done.3, f32[4,256]{1,0:T(4,128)S(1)} %collective-permute-done.1, f32[4096,255]{1,0:T(8,128)} %bitcast.26, f32[4096,1]{1,0:T(8,128)S(1)} %copy.10, bf16[4096,256]{1,0:T(8,128)(2,1)} %param.15, f32[4096]{0:T(1024)S(1)} %copy-done.2, ...), kind=kLoop, calls=%fused_computation.16 | loop fusion | flops 42991616 | bytes 14852096 | tf_op jit(solution)/shard_map/sub | solution.py:71
  82.9 0.0 copy-start.1
  82.9 0.6 slice_reduce_fusion
  83.5 1.3 collective-permute-start.5
  84.8 3.6 %collective-permute-start.6 = (f32[4,256]{1,0:T(4,128)S(1)}, f32[4,256]{1,0:T(4,128)S(1)}, u32[]{:S(2)}, u32[]{:S(2)}) collective-permute-start(f32[4,256]{1,0:T(4,128)S(1)} %get-tuple-element.3), channel_id=1, source_target_pairs={{0,8},{8,16},{16,24},{1,9},{9,17},{17,25},{2,10},{10,18},{18,26},{... | collective-permute-start | bytes 12296 | tf_op jit(solution)/shard_map/ppermute | solution.py:24
  88.4 1.3 collective-permute-start.4
  89.7 3.1 %slice.177 = f32[4096,255]{1,0:T(8,128)} slice(f32[4096,256]{1,0:T(8,128)S(1)} %fusion.1), slice={[0:4096], [1:256]} | slice | bytes 8355840 | tf_op jit(solution)/shard_map/slice | solution.py:77
  92.8 0.0 copy-done.1
  92.8 1.2 collective-permute-done.4
  94.0 2.0 copy.11
  96.0 0.0 collective-permute-done.5
  96.0 0.0 collective-permute-done.6
  96.0 21.7 %fusion.4 = bf16[4096,256]{1,0:T(8,128)(2,1)S(1)} fusion(f32[4096,256]{1,0:T(8,128)} %copy-done.1, f32[4096,256]{1,0:T(8,128)} %copy-done, f32[4,256]{1,0:T(4,128)S(1)} %collective-permute-done.6, f32[4,256]{1,0:T(4,128)S(1)} %collective-permute-done.5, f32[4096,1]{1,0:T(8,128)} %copy.11, f32[4096,255]{1,0:T(8,128)} %slice.177, ...), kind=kLoop, calls=%fused_computation.19 | loop fusion | flops 41943040 | bytes 14852096 | tf_op jit(solution)/shard_map/convert_element_type | solution.py:84
  117.7 1.1 convolution_bitcast_fusion.1
  118.8 0.0 reduce-scatter.5.cloned.1.call-update
  118.8 0.0 reduce-scatter.3.cloned.1.call-start
  118.9 1.7 convolution_bitcast_fusion
  120.6 0.0 reduce-scatter.3.cloned.1.call-update
  120.6 16.7 %reduce-scatter.5.cloned.1.call-done = f32[16,256]{1,0:T(8,128)} async-done(((f32[64,256]{1,0:T(8,128)}), f32[16,256]{1,0:T(8,128)}) %reduce-scatter.5.cloned.1.call-update) | async-done | bytes 16400 | tf_op jit(solution)/shard_map/reduce_scatter | solution.py:97
  137.3 1.3 broadcast_multiply_fusion.1
  138.6 65.9 %reduce-scatter.3.cloned.1.call-done = f32[8,4096]{1,0:T(8,128)} async-done(((f32[64,4096]{1,0:T(8,128)}), f32[8,4096]{1,0:T(8,128)}) %reduce-scatter.3.cloned.1.call-update) | async-done | bytes 131088 | tf_op jit(solution)/shard_map/reduce_scatter | solution.py:88
  204.5 1.6 broadcast_multiply_fusion
  (5 shorter events, 0.0 us)
Async XLA Ops:
  7.2 52.9 %copy-start.4 = (f32[4096]{0:T(1024)S(1)}, f32[4096]{0:T(1024)}, u32[]{:S(2)}) copy-start(f32[4096]{0:T(1024)} %param.10) | copy-start | bytes 49156
  7.2 130.1 %reduce-scatter.5.cloned.1.call-start = ((), (), s32[]{:S(2)}) async-start(), calls=%async_computation.3 | async-start | bytes 81920 | tf_op jit(solution)/shard_map/reduce_scatter | solution.py:97
  13.8 46.1 %collective-permute-start = (bf16[64]{0:T(256)(128)(2,1)S(1)}, bf16[64]{0:T(256)(128)(2,1)S(1)}, u32[]{:S(2)}, u32[]{:S(2)}) collective-permute-start(bf16[64]{0:T(256)(128)(2,1)S(1)} %slice_reduce_fusion.1), channel_id=1, source_target_pairs={{0,1},{1,2},{2,3},{3,4},{4,5},{5,6},{6,7},{8,9},{9,10},{10,11},{11... | collective-permute-start | bytes 392 | tf_op jit(solution)/shard_map/ppermute | solution.py:14
  18.5 42.3 %copy-start.2 = (f32[4096]{0:T(1024)S(1)}, f32[4096]{0:T(1024)}, u32[]{:S(2)}) copy-start(f32[4096]{0:T(1024)} %param.14) | copy-start | bytes 49156
  18.5 42.3 %copy-start.3 = (f32[4096]{0:T(1024)S(1)}, f32[4096]{0:T(1024)}, u32[]{:S(2)}) copy-start(f32[4096]{0:T(1024)} %param.13) | copy-start | bytes 49156
  18.6 41.1 %collective-permute-start.2 = (f32[4,4]{1,0:T(4,128)S(1)}, f32[4,4]{1,0:T(4,128)S(1)}, u32[]{:S(2)}, u32[]{:S(2)}) collective-permute-start(f32[4,4]{1,0:T(4,128)S(1)} %slice.162), channel_id=1, source_target_pairs={{0,8},{8,16},{16,24},{1,9},{9,17},{17,25},{2,10},{10,18},{18,26},{... | collective-permute-start | bytes 200 | tf_op jit(solution)/shard_map/ppermute | solution.py:14
  53.4 1.9 copy-start
  55.3 5.4 %collective-permute-start.1 = (f32[4,256]{1,0:T(4,128)S(1)}, f32[4,256]{1,0:T(4,128)S(1)}, u32[]{:S(2)}, u32[]{:S(2)}) collective-permute-start(f32[4,256]{1,0:T(4,128)S(1)} %get-tuple-element.4), channel_id=1, source_target_pairs={{8,0},{16,8},{24,16},{9,1},{17,9},{25,17},{10,2},{18,10},{26,18},{... | collective-permute-start | bytes 12296 | tf_op jit(solution)/shard_map/ppermute | solution.py:25
  56.6 4.1 %collective-permute-start.3 = (f32[4,256]{1,0:T(4,128)S(1)}, f32[4,256]{1,0:T(4,128)S(1)}, u32[]{:S(2)}, u32[]{:S(2)}) collective-permute-start(f32[4,256]{1,0:T(4,128)S(1)} %get-tuple-element.5), channel_id=1, source_target_pairs={{0,8},{8,16},{16,24},{1,9},{9,17},{17,25},{2,10},{10,18},{18,26},{... | collective-permute-start | bytes 12296 | tf_op jit(solution)/shard_map/ppermute | solution.py:24
  82.9 10.0 %copy-start.1 = (f32[4096,256]{1,0:T(8,128)}, f32[4096,256]{1,0:T(8,128)S(1)}, u32[]{:S(2)}) copy-start(f32[4096,256]{1,0:T(8,128)S(1)} %fusion.1) | copy-start | bytes 12582916
  83.5 12.5 %collective-permute-start.5 = (f32[4,256]{1,0:T(4,128)S(1)}, f32[4,256]{1,0:T(4,128)S(1)}, u32[]{:S(2)}, u32[]{:S(2)}) collective-permute-start(f32[4,256]{1,0:T(4,128)S(1)} %get-tuple-element.2), channel_id=1, source_target_pairs={{8,0},{16,8},{24,16},{9,1},{17,9},{25,17},{10,2},{18,10},{26,18},{... | collective-permute-start | bytes 12296 | tf_op jit(solution)/shard_map/ppermute | solution.py:25
  84.8 11.2 %collective-permute-start.6 = (f32[4,256]{1,0:T(4,128)S(1)}, f32[4,256]{1,0:T(4,128)S(1)}, u32[]{:S(2)}, u32[]{:S(2)}) collective-permute-start(f32[4,256]{1,0:T(4,128)S(1)} %get-tuple-element.3), channel_id=1, source_target_pairs={{0,8},{8,16},{16,24},{1,9},{9,17},{17,25},{2,10},{10,18},{18,26},{... | collective-permute-start | bytes 12296 | tf_op jit(solution)/shard_map/ppermute | solution.py:24
  88.4 5.6 %collective-permute-start.4 = (f32[4096]{0:T(1024)S(1)}, f32[4096]{0:T(1024)S(1)}, u32[]{:S(2)}, u32[]{:S(2)}) collective-permute-start(f32[4096]{0:T(1024)S(1)} %slice_reduce_fusion), channel_id=1, source_target_pairs={{1,0},{2,1},{3,2},{4,3},{5,4},{6,5},{7,6},{9,8},{10,9},{11,10},{12... | collective-permute-start | bytes 49160 | tf_op jit(solution)/shard_map/ppermute | solution.py:14
  118.8 85.7 %reduce-scatter.3.cloned.1.call-start = ((), (), s32[]{:S(2)}) async-start(), calls=%async_computation.2 | async-start | bytes 1179648 | tf_op jit(solution)/shard_map/reduce_scatter | solution.py:88
Sparse Core Ops, SparseCore 0:
  118.9 18.3 reduce-scatter.4
  141.1 63.3 reduce-scatter.2
where the time goes:
time: 214 us; the launch traced here: 213 us
  waiting for transfers between devices  83.8 us (39%)
  other arithmetic  47.7 us (22%)
  blocking collectives  38.5 us (18%)
  starting transfers between devices  16.3 us (8%)
  between operations  14.3 us (7%)
  local copies, waits for them, and re-layouts  8.57 us (4%)
  matrix products  3.73 us (2%)
    reduce_scatter x1, waiting for transfers between devices, body(): lax.psum_scatter(lax.dot_general(picked, descent_b, (((1,), (1,)), ((), (...  65.9 us
    all_gather x1, blocking collectives, body(): space_full = lax.all_gather(space_factor, 'tm', axis=0, tiled=True)  32.1 us
    sub x1, other arithmetic, body(): mass_col * (state - earlier) + diffuse(padded, rates_padded, node_count)  22.1 us
    convert_element_type x1, other arithmetic, body(): descent_b = descent.astype(jnp.bfloat16)  21.7 us
    reduce_scatter x1, waiting for transfers between devices, body(): lax.psum_scatter(jnp.dot(picked, descent_b, preferred_element_type=jnp.fl...  16.7 us
    ppermute x3, starting transfers between devices, from_behind(): return lax.ppermute(array, axis, pairs)  7.06 us
    ppermute x2, starting transfers between devices, padded_2(): before = lax.ppermute(last, axis, up)  6.61 us
    all_gather x1, blocking collectives, body(): time_full = lax.all_gather(time_factor, 'space', axis=0, tiled=True)  6.42 us
  transfers between devices with their start and end apart: 9, of which 3 were waited for; matrix products, arithmetic and copies ran while one was open for 5% of the time, Pallas kernels for 0%

commit v1 on v0

--- a/solution.py
+++ b/solution.py
@@ -1,11 +1,18 @@
+import functools
 import math
 
 import jax
 import jax.numpy as jnp
 from jax import lax
+from jax.experimental import pallas as pl
+from jax.experimental.pallas import tpu as pltpu
 from jax.sharding import PartitionSpec as P
 
 W = 4
+LANES = 128
+CHUNK = 512
+LAG = 2
+MESH = pl.DeviceIdType.MESH
 
 
 def from_behind(array, axis, by):
@@ -104,6 +111,412 @@
     return (grad_space, grad_time)
 
 
+def fused_kernel(
+    n_space, n_tm, chunk,
+    space_ref, time_ref, vec_ref, source_ref,
+    grad_space_ref, grad_time_ref,
+    src_v, s_all, t_all, t_prev, s_ext, edge_out, edge_in, coef, g1, g23, gedge_out, gedge_in,
+    h1, h2, weights, pair, u_send, u_recv, e_send, e_recv,
+    part, part_in, zsum, z_in, total,
+    src_sem, t_send, t_got, tp_sem, s_send, s_got, edge_send, edge_got,
+    gedge_send, gedge_got, u_ss, u_rs, e_ss, e_rs, x_ss, x_rs, z_ss, z_rs,
+):
+    f32, bf16 = jnp.float32, jnp.bfloat16
+    s, m = lax.axis_index("space"), lax.axis_index("tm")
+    n_z = n_tm // 2
+    z, x = lax.div(m, 2), lax.rem(m, 2)
+    nodes, steps = source_ref.shape
+    half = nodes // 2
+    rows = space_ref.shape[0]
+    rank = rows * n_tm
+    t_rows = time_ref.shape[0]
+    count = nodes // chunk
+    wide = chunk + 2 * LANES
+
+    def dev(space, tm):
+        return {"space": space, "tm": tm}
+
+    def send(src, dst, ss, rs, space, tm):
+        return pltpu.make_async_remote_copy(
+            src_ref=src, dst_ref=dst, send_sem=ss, recv_sem=rs,
+            device_id=dev(space, tm), device_id_type=MESH,
+        )
+
+    load = pltpu.make_async_copy(source_ref, src_v, src_sem)
+    load.start()
+    edge_in[...] = jnp.zeros_like(edge_in)
+    gedge_in[...] = jnp.zeros_like(gedge_in)
+
+    barrier = pltpu.get_barrier_semaphore()
+
+    def greet(space, tm):
+        pl.semaphore_signal(barrier, inc=1, device_id=dev(space, tm), device_id_type=MESH)
+
+    for k in range(1, n_space):
+        greet(lax.rem(s + k, n_space), m)
+    for k in range(1, n_z):
+        greet(s, lax.rem(z + k, n_z) * 2 + x)
+    greet(s, z * 2 + 1 - x)
+
+    @pl.when(m > 0)
+    def _():
+        for k in range(n_space):
+            greet(k, lax.rem(m + n_tm - 1, n_tm))
+
+    @pl.when(m < n_tm - 1)
+    def _():
+        for k in range(n_space):
+            greet(k, lax.rem(m + 1, n_tm))
+
+    first = space_ref[...].astype(f32)
+    s_all[m] = jnp.concatenate([first[:, :half], first[:, half:]], axis=0).astype(bf16)
+    t_all[s] = time_ref[...]
+    expected = (n_space - 1) + (n_z - 1) + 1
+    expected = expected + jnp.where(m > 0, n_space, 0) + jnp.where(m < n_tm - 1, n_space, 0)
+    pl.semaphore_wait(barrier, expected)
+
+    def t_copy(k):
+        return send(t_all.at[s], t_all.at[s], t_send.at[k], t_got.at[k], lax.rem(s + k, n_space), m)
+
+    def s_copy(k):
+        return send(s_all.at[m], s_all.at[m], s_send.at[k], s_got.at[k], s, lax.rem(z + k, n_z) * 2 + x)
+
+    def x_copy(k):
+        owner = lax.rem(z + n_z - k, n_z) * 2 + x
+        return send(s_all.at[owner], s_all.at[owner], s_send.at[n_z + k], s_got.at[n_z + k], s, z * 2 + 1 - x)
+
+    for k in range(1, n_space):
+        t_copy(k).start()
+    x_copy(0).start()
+    for k in range(1, n_z):
+        s_copy(k).start()
+
+    link = vec_ref[0:1, :]
+    cond = vec_ref[1:2, :]
+    mass = vec_ref[2:3, :LANES + nodes][:, LANES:]
+    diag = mass
+    for d in range(1, W + 1):
+        rate = jnp.where(link == d, cond, 0.0)
+        own = rate[:, LANES:]
+        came = pltpu.roll(rate, d, 1)[:, LANES:]
+        coef[d - 1:d, :] = own
+        coef[W + d - 1:W + d, :] = came
+        diag = diag + own + came
+    coef[8:9, :] = diag
+    coef[9:10, :] = mass
+    coef[16:17, :] = vec_ref[3:4, LANES:]
+    lead = jnp.where(m == 0, 1.0, 0.0)
+    coef[17:18, :] = mass * vec_ref[4:5, LANES:] * lead
+    coef[18:24, :] = jnp.zeros((6, nodes), f32)
+    h1[...] = jnp.zeros_like(h1)
+    h2[...] = jnp.zeros_like(h2)
+
+    for k in range(1, n_space):
+        t_copy(k).wait()
+
+    t_edge = send(t_all.at[:, :, pl.ds(steps - LANES, LANES)], t_prev, tp_sem.at[0], tp_sem.at[1], s, lax.rem(m + 1, n_tm))
+
+    @pl.when(m < n_tm - 1)
+    def _():
+        t_edge.start()
+
+    for k in range(1, n_z):
+        s_copy(k).wait_recv()
+        x_copy(k).start()
+
+    @pl.when(m < n_tm - 1)
+    def _():
+        t_edge.wait_send()
+
+    @pl.when(m > 0)
+    def _():
+        t_edge.wait_recv()
+
+    @pl.when(m == 0)
+    def _():
+        t_prev[...] = jnp.zeros_like(t_prev)
+
+    t_full = t_all[...].reshape(rank, steps)
+    tf = t_full.astype(f32)
+    prev = t_prev[...].reshape(rank, LANES).astype(f32)
+    lane = lax.broadcasted_iota(jnp.int32, (rank, steps), 1)
+    prev = pltpu.roll(prev, 1, 1)
+    prev = jnp.concatenate([prev] + [jnp.zeros_like(prev)] * (steps // LANES - 1), axis=1)
+    minus = -jnp.where(lane == 0, prev, pltpu.roll(tf, 1, 1))
+    minus = minus.astype(bf16)
+    weights[...] = jnp.concatenate([t_full, t_full, minus, minus], axis=0)
+    pair[...] = jnp.concatenate([t_full, minus], axis=0)
+
+    for k in range(1, n_z):
+        s_copy(k).wait_send()
+    for k in range(n_z):
+        x_copy(k).wait()
+
+    for k in range(n_tm):
+        block = s_all[k].astype(f32)
+        s_ext[k * rows:(k + 1) * rows, LANES:LANES + half] = block[:rows]
+        s_ext[k * rows:(k + 1) * rows, LANES + half:LANES + nodes] = block[rows:]
+
+    edge_out[0] = s_ext[:, LANES:2 * LANES].astype(bf16)
+    edge_out[1] = s_ext[:, nodes:LANES + nodes].astype(bf16)
+
+    def edge_copies(out, inn, ss, rs):
+        down = send(out.at[0], inn.at[0], ss.at[0], rs.at[0], lax.rem(s + n_space - 1, n_space), m)
+        up = send(out.at[1], inn.at[1], ss.at[1], rs.at[1], lax.rem(s + 1, n_space), m)
+        return down, up
+
+    def edges_start(down, up):
+        @pl.when(s > 0)
+        def _():
+            down.start()
+
+        @pl.when(s < n_space - 1)
+        def _():
+            up.start()
+
+    def edges_wait(down, up):
+        @pl.when(s > 0)
+        def _():
+            down.wait_send()
+            up.wait_recv()
+
+        @pl.when(s < n_space - 1)
+        def _():
+            up.wait_send()
+            down.wait_recv()
+
+    s_edges = edge_copies(edge_out, edge_in, edge_send, edge_got)
+    edges_start(*s_edges)
+    s_ext[:, 0:LANES] = jnp.zeros((rank, LANES), f32)
+    s_ext[:, LANES + nodes:] = jnp.zeros((rank, LANES), f32)
+
+    def banded(field, at):
+        out = coef[8:9, pl.ds(at, chunk)] * field[:, LANES:LANES + chunk]
+        for d in range(1, W + 1):
+            ahead = pltpu.roll(field, wide - d, 1)[:, LANES:LANES + chunk]
+            behind = pltpu.roll(field, d, 1)[:, LANES:LANES + chunk]
+            out = out - coef[d - 1:d, pl.ds(at, chunk)] * ahead
+            out = out - coef[W + d - 1:W + d, pl.ds(at, chunk)] * behind
+        return out
+
+    def split(v):
+        high = v.astype(bf16)
+        return high, (v - high.astype(f32)).astype(bf16)
+
+    def dot_t(a, b):
+        return lax.dot_general(a, b, (((0,), (0,)), ((), ())), preferred_element_type=f32)
+
+    def dot_n(a, b):
+        return lax.dot_general(a, b, (((1,), (0,)), ((), ())), preferred_element_type=f32)
+
+    def dot_r(a, b):
+        return lax.dot_general(a, b, (((1,), (1,)), ((), ())), preferred_element_type=f32)
+
+    load.wait()
+    e0 = jnp.where(lax.broadcasted_iota(jnp.int32, (1, steps), 1) == 0, 1.0, 0.0)
+
+    def forward(i, carry):
+        c = lax.rem(i + 1, count)
+        at = pl.multiple_of(c * chunk, chunk)
+
+        @pl.when(i == count - 2)
+        def _():
+            edges_wait(*s_edges)
+            s_ext[:, 0:LANES] = edge_in[1].astype(f32)
+            s_ext[:, LANES + nodes:] = edge_in[0].astype(f32)
+
+        field = s_ext[:, pl.ds(at, wide)]
+        mid = field[:, LANES:LANES + chunk]
+        mass_c = coef[9:10, pl.ds(at, chunk)]
+        a_hi, a_lo = split(banded(field, at))
+        b_hi, b_lo = split(mass_c * mid)
+        left = jnp.concatenate([a_hi, a_lo, b_hi, b_lo], axis=0)
+        s_b = mid.astype(bf16)
+        cols = coef[16:24, pl.ds(at, chunk)].T
+        lin = dot_t(left, weights[...])
+        state = dot_t(s_b, pair[0:rank, :])
+        cube = cols[:, 0:1] * state * state
+        res = lin + cube * state - src_v[pl.ds(at, chunk), :].astype(f32) - cols[:, 1:2] * e0
+        q = (3.0 * cube * res).astype(bf16)
+        r_hi, r_lo = split(res)
+        big = dot_n(left, r_hi)
+        small = dot_n(jnp.concatenate([a_hi, b_hi], axis=0), r_lo)
+        h1[...] += big[:rank] + big[rank:2 * rank] + small[:rank] + dot_n(s_b, q)
+        h2[...] += big[2 * rank:3 * rank] + big[3 * rank:] + small[rank:]
+        g = dot_r(pair[...], r_hi) + dot_r(pair[...], r_lo)
+        gq = dot_r(pair[0:rank, :], q)
+        g1[:, pl.ds(pl.multiple_of(at + LANES, LANES), chunk)] = g[:rank]
+        g23[:, pl.ds(at, chunk)] = mass_c * g[rank:] + gq
+        return carry
+
+    lax.fori_loop(0, count, forward, 0)
+
+    gedge_out[0] = g1[:, LANES:2 * LANES]
+    gedge_out[1] = g1[:, nodes:LANES + nodes]
+    g_edges = edge_copies(gedge_out, gedge_in, gedge_send, gedge_got)
+    edges_start(*g_edges)
+    g1[:, 0:LANES] = jnp.zeros((rank, LANES), f32)
+    g1[:, LANES + nodes:] = jnp.zeros((rank, LANES), f32)
+
+    h2v = h2[...]
+    shifted = jnp.where(lane == steps - 1, 0.0, pltpu.roll(h2v, steps - 1, 1))
+    share = h1[...] - shifted
+    for k in range(n_space):
+        u_send[k] = share[k * t_rows:(k + 1) * t_rows]
+        e_send[k] = h2v[k * t_rows:(k + 1) * t_rows, :LANES]
+
+    def u_copy(k):
+        to = lax.rem(s + k, n_space)
+        return send(u_send.at[to], u_recv.at[s], u_ss.at[k], u_rs.at[k], to, m)
+
+    def e_copy(k):
+        to = lax.rem(s + k, n_space)
+        return send(e_send.at[to], e_recv.at[s], e_ss.at[k], e_rs.at[k], to, lax.rem(m + n_tm - 1, n_tm))
+
+    scale = 1.0 / math.sqrt(steps * n_tm)
+
+    def x_part(c):
+        return send(part.at[1 - x, c], part_in.at[c], x_ss.at[c], x_rs.at[c], s, z * 2 + 1 - x)
+
+    def z_part(c, k):
+        to = lax.rem(z + k, n_z)
+        return send(zsum.at[c, to], z_in.at[c, z], z_ss.at[c, k], z_rs.at[c, k], s, to * 2 + x)
+
+    def combine(c):
+        x_part(c).wait_recv()
+        both = part[x, c] + part_in[c]
+        for k in range(n_z):
+            zsum[c, k] = both[k * rows:(k + 1) * rows]
+        for k in range(1, n_z):
+            z_part(c, k).start()
+
+    def backward(i, carry):
+        c = lax.rem(i + 1, count)
+        at = pl.multiple_of(c * chunk, chunk)
+
+        @pl.when(i == count - 2)
+        def _():
+            edges_wait(*g_edges)
+            g1[:, 0:LANES] = gedge_in[1]
+            g1[:, LANES + nodes:] = gedge_in[0]
+
+        out = (banded(g1[:, pl.ds(at, wide)], at) + g23[:, pl.ds(at, chunk)]) * scale
+        for side in range(2):
+            part[side, c] = jnp.concatenate(
+                [out[(2 * k + side) * rows:(2 * k + side + 1) * rows] for k in range(n_z)], axis=0
+            )
+        x_part(c).start()
+
+        @pl.when(i >= LAG)
+        def _():
+            combine(lax.rem(i - LAG + 1 + count, count))
+
+        return carry
+
+    lax.fori_loop(0, count, backward, 0)
+
+    for k in range(1, n_space):
+        u_copy(k).start()
+
+    @pl.when(m > 0)
+    def _():
+        for k in range(n_space):
+            e_copy(k).start()
+
+    for i in range(count - LAG, count):
+        combine((i + 1) % count)
+
+    for k in range(1, n_space):
+        u_copy(k).wait()
+
+    @pl.when(m > 0)
+    def _():
+        for k in range(n_space):
+            e_copy(k).wait_send()
+
+    @pl.when(m < n_tm - 1)
+    def _():
+        for k in range(n_space):
+            e_copy(k).wait_recv()
+
+    @pl.when(m == n_tm - 1)
+    def _():
+        e_recv[...] = jnp.zeros_like(e_recv)
+
+    mine = u_send[s]
+    for k in range(1, n_space):
+        mine = mine + u_recv[lax.rem(s + k, n_space)]
+    edge = e_recv[0]
+    for k in range(1, n_space):
+        edge = edge + e_recv[k]
+    at_end = lax.broadcasted_iota(jnp.int32, (t_rows, LANES), 1) == LANES - 1
+    edge = jnp.where(at_end, pltpu.roll(edge, LANES - 1, 1), 0.0)
+    edge = jnp.concatenate([jnp.zeros((t_rows, steps - LANES), f32), edge], axis=1)
+    grad_time_ref[...] = (mine - edge) * (1.0 / math.sqrt(nodes * n_space))
+
+    def finish(i, carry):
+        c = lax.rem(i + 1, count)
+        at = pl.multiple_of(c * chunk, chunk)
+        total_c = zsum[c, z]
+        for k in range(1, n_z):
+            z_part(c, k).wait()
+            total_c = total_c + z_in[c, lax.rem(z + n_z - k, n_z)]
+        x_part(c).wait_send()
+        grad_space_ref[:, pl.ds(at, chunk)] = total_c
+        return carry
+
+    lax.fori_loop(0, count, finish, 0)
+
+
+def fused(n_space, n_tm, space_factor, time_factor, initial_state, link, conductivity, mass, reaction, source):
+    f32, bf16 = jnp.float32, jnp.bfloat16
+    nodes, steps = source.shape
+    rows, t_rows = space_factor.shape[0], time_factor.shape[0]
+    rank = rows * n_tm
+    chunk = CHUNK
+    count = nodes // chunk
+    n_z = n_tm // 2
+    ends = jnp.stack([link[nodes - LANES:].astype(f32), conductivity[nodes - LANES:]])
+    ends = from_behind(ends, "space", 1)
+    body = jnp.stack([link.astype(f32), conductivity, mass, reaction, initial_state])
+    vec = jnp.concatenate([jnp.pad(ends, ((0, 3), (0, 0))), body], axis=1)
+    vec = jnp.pad(vec, ((0, 3), (0, 0)))
+    dma, V = pltpu.SemaphoreType.DMA, pltpu.VMEM
+    scratch = [
+        V((nodes, steps), bf16), V((n_tm, 2 * rows, nodes // 2), bf16),
+        V((n_space, t_rows, steps), bf16), V((n_space, t_rows, LANES), bf16),
+        V((rank, nodes + 2 * LANES), f32), V((2, rank, LANES), bf16), V((2, rank, LANES), bf16),
+        V((24, nodes), f32), V((rank, nodes + 2 * LANES), f32), V((rank, nodes), f32),
+        V((2, rank, LANES), f32), V((2, rank, LANES), f32),
+        V((rank, steps), f32), V((rank, steps), f32),
+        V((4 * rank, steps), bf16), V((2 * rank, steps), bf16),
+        V((n_space, t_rows, steps), f32), V((n_space, t_rows, steps), f32),
+        V((n_space, t_rows, LANES), f32), V((n_space, t_rows, LANES), f32),
+        V((2, count, n_z * rows, chunk), f32), V((count, n_z * rows, chunk), f32),
+        V((count, n_z, rows, chunk), f32), V((count, n_z, rows, chunk), f32),
+        V((8, LANES), f32),
+        dma, dma((n_space,)), dma((n_space,)), dma((2,)), dma((2 * n_z,)), dma((2 * n_z,)),
+        dma((2,)), dma((2,)), dma((2,)), dma((2,)),
+        dma((n_space,)), dma((n_space,)), dma((n_space,)), dma((n_space,)),
+        dma((count,)), dma((count,)), dma((count, n_z)), dma((count, n_z)),
+    ]
+    vm = pl.BlockSpec(memory_space=pltpu.VMEM)
+    return pl.pallas_call(
+        functools.partial(fused_kernel, n_space, n_tm, chunk),
+        out_shape=(
+            jax.ShapeDtypeStruct((rows, nodes), f32),
+            jax.ShapeDtypeStruct((t_rows, steps), f32),
+        ),
+        in_specs=[vm, vm, vm, pl.BlockSpec(memory_space=pl.ANY)],
+        out_specs=(vm, vm),
+        scratch_shapes=scratch,
+        compiler_params=pltpu.CompilerParams(
+            collective_id=0, has_side_effects=True, vmem_limit_bytes=48 * 1024 * 1024
+        ),
+        name="fused",
+    )(space_factor, time_factor, vec, source)
+
+
 def solution(mesh):
     in_specs = (
         P("tm", "space"),
@@ -116,4 +529,16 @@
         P("space", "tm"),
     )
     out_specs = (P("tm", "space"), P("space", "tm"))
-    return jax.shard_map(body, mesh=mesh, in_specs=in_specs, out_specs=out_specs, check_vma=False)
+    n_space, n_tm = mesh.shape["space"], mesh.shape["tm"]
+
+    def run(space_factor, time_factor, *rest):
+        nodes, steps = rest[-1].shape
+        fits = (
+            space_factor.shape[0] % 8 == 0 and time_factor.shape[0] % 16 == 0 and n_tm % 2 == 0
+            and nodes % (2 * CHUNK) == 0 and nodes >= 4 * CHUNK and steps % LANES == 0
+        )
+        if fits:
+            return fused(n_space, n_tm, space_factor, time_factor, *rest)
+        return body(space_factor, time_factor, *rest)
+
+    return jax.shard_map(run, mesh=mesh, in_specs=in_specs, out_specs=out_specs, check_vma=False)

time: 214 us -> 59 us (0.28)
  waiting for transfers between devices: 83.8 us -> 0.01 us
  Pallas kernels: 0 us -> 48 us
  other arithmetic: 47.7 us -> 1.44 us
  blocking collectives: 38.5 us -> 0 us
  starting transfers between devices: 16.3 us -> 2.35 us
  between operations: 14.3 us -> 0.68 us
  matrix products: 3.73 us -> 0 us
  local copies, waits for them, and re-layouts: 8.57 us -> 5.98 us
    reduce_scatter x2 -> x0, waiting for transfers between devices: 82.6 us -> none  [the longest x1 65.9 us: body(): lax.psum_scatter(lax.dot_general(picked, descent_b, (((1,), (1,)), ((), (...]
    pallas_call x0 -> x1, Pallas kernels: none -> 48 us  [fused(): pl.pallas_call(functools.partial(fused_kernel, n_space, n_tm, chunk), out...]
    all_gather x2 -> x0, blocking collectives: 38.5 us -> none  [the longest x1 32.1 us: body(): space_full = lax.all_gather(space_factor, 'tm', axis=0, tiled=True)]
    sub x1 -> x0, other arithmetic: 22.1 us -> none  [body(): mass_col * (state - earlier) + diffuse(padded, rates_padded, node_count)]
    convert_element_type x1, other arithmetic: 21.7 us -> 0.72 us  [fused(): link.astype(f32)]
    ppermute x4 -> x0, starting transfers between devices: 9.18 us -> none  [the longest x2 6.61 us: padded_2(): before = lax.ppermute(last, axis, up)]
    ppermute x3 -> x1, starting transfers between devices: 7.06 us -> 2.35 us  [from_behind(): return lax.ppermute(array, axis, pairs)]
    slice x6 -> x0, local copies, waits for them, and re-layouts: 3.98 us -> none  [the longest x1 3.12 us: body(): later = jnp.concatenate([residual[:, 1:], following[:, None]], axis=1)]
  transfers between devices with their start and end apart: 9 -> 1, of which waited for: 3 -> 0; matrix products, arithmetic and copies ran while one was open for 5% -> 3% of each run, Pallas kernels for 0% -> 0%
where the time goes in v1:
time: 59 us; the launch traced here: 58.4 us
  Pallas kernels  48 us (81%)
  local copies, waits for them, and re-layouts  5.98 us (10%)
  starting transfers between devices  2.35 us (4%)
  other arithmetic  1.44 us (2%)
  between operations  0.68 us (1%)
    pallas_call x1, Pallas kernels, fused(): pl.pallas_call(functools.partial(fused_kernel, n_space, n_tm, chunk), out...  48 us
    unnamed x8, local copies, waits for them, and re-layouts  4.38 us
    ppermute x1, starting transfers between devices, from_behind(): return lax.ppermute(array, axis, pairs)  2.35 us
  transfers between devices with their start and end apart: 1, of which 0 were waited for; matrix products, arithmetic and copies ran while one was open for 3% of the time, Pallas kernels for 0%

profile of v1, /device:TPU:0, one launch (start us, length us, event | category | flops | bytes accessed | tf_op | source)
XLA Modules:
  0.0 58.4 jit_solution(16690094626434630777)
XLA Ops:
  0.6 0.7 %convert_bitcast_fusion = f32[1,128]{1,0:T(1,128)S(1)} fusion(s32[4096]{0:T(1024)} %param.11), kind=kLoop, calls=%fused_computation.4 | loop fusion | flops 128 | bytes 1024 | tf_op jit(solution)/shard_map/stack | solution.py:479
  1.3 0.7 %slice_bitcast_fusion = f32[1,128]{1,0:T(1,128)S(1)} fusion(f32[4096]{0:T(1024)} %param.12), kind=kLoop, calls=%fused_computation.3 | loop fusion | bytes 1024 | tf_op jit(solution)/shard_map/stack | solution.py:479
  2.0 2.4 %collective-permute-start = (f32[2,128]{1,0:T(2,128)S(1)}, f32[2,128]{1,0:T(2,128)S(1)}, u32[]{:S(2)}, u32[]{:S(2)}) collective-permute-start(f32[2,128]{1,0:T(2,128)S(1)} %pad_maximum_fusion), channel_id=1, source_target_pairs={{0,8},{8,16},{16,24},{1,9},{9,17},{17,25},{2,10},{10,18},{18,26},{... | collective-permute-start | bytes 3080 | tf_op jit(solution)/shard_map/ppermute | solution.py:21
  4.4 0.7 %convert_element_type.11 = f32[4096]{0:T(1024)S(1)} convert(s32[4096]{0:T(1024)} %param.11) | non-fusion elementwise | flops 4096 | bytes 32768 | tf_op jit(solution)/shard_map/convert_element_type | solution.py:481
  5.1 0.9 %stack.35 = f32[5,4096]{1,0:T(8,128)S(1)} concatenate(f32[1,4096]{1,0:T(1,128)S(1)} %bitcast.9, f32[1,4096]{1,0:T(1,128)} %bitcast.10, f32[1,4096]{1,0:T(1,128)} %bitcast.11, f32[1,4096]{1,0:T(1,128)} %bitcast.12, f32[1,4096]{1,0:T(1,128)} %bitcast.13), dimensions={0} | concatenate | bytes 163840 | tf_op jit(solution)/shard_map/stack | solution.py:481
  6.0 0.0 collective-permute-done
  6.1 0.0 copy-start
  6.1 1.6 %copy-done = bf16[4096,256]{1,0:T(8,128)(2,1)S(1)} copy-done((bf16[4096,256]{1,0:T(8,128)(2,1)S(1)}, bf16[4096,256]{1,0:T(8,128)(2,1)}, u32[]{:S(2)}) %copy-start) | copy-done | bytes 2097176
  7.7 0.0 copy-start.1
  7.7 0.8 %copy-done.1 = bf16[8,4096]{1,0:T(8,128)(2,1)S(1)} copy-done((bf16[8,4096]{1,0:T(8,128)(2,1)S(1)}, bf16[8,4096]{1,0:T(8,128)(2,1)}, u32[]{:S(2)}) %copy-start.1) | copy-done | bytes 65560
  8.5 0.0 copy-start.2
  8.5 0.7 %copy-done.2 = bf16[16,256]{1,0:T(8,128)(2,1)S(1)} copy-done((bf16[16,256]{1,0:T(8,128)(2,1)S(1)}, bf16[16,256]{1,0:T(8,128)(2,1)}, u32[]{:S(2)}) %copy-start.2) | copy-done | bytes 8216
  9.2 48.0 %fused.1 = (f32[8,4096]{1,0:T(8,128)S(1)}, f32[16,256]{1,0:T(8,128)S(1)}) custom-call(bf16[8,4096]{1,0:T(8,128)(2,1)S(1)} %copy-done.1, bf16[16,256]{1,0:T(8,128)(2,1)S(1)} %copy-done.2, f32[8,4224]{1,0:T(8,128)S(1)} %pad.9.vec_ref, bf16[4096,256]{1,0:T(8,128)(2,1)S(1)} %copy-done), custom_call_target="tpu_custom_call" | custom-call | tf_op jit(solution)/shard_map/fused/pallas_call | solution.py:504
  57.2 0.7 %copy.12 = f32[8,4096]{1,0:T(8,128)} copy(f32[8,4096]{1,0:T(8,128)S(1)} %get-tuple-element.4) | data formatting | bytes 262144
  57.8 0.6 %copy.13 = f32[16,256]{1,0:T(8,128)} copy(f32[16,256]{1,0:T(8,128)S(1)} %get-tuple-element.5) | data formatting | bytes 32768
  (3 shorter events, 0.0 us)
Async XLA Ops:
  2.0 4.0 %collective-permute-start = (f32[2,128]{1,0:T(2,128)S(1)}, f32[2,128]{1,0:T(2,128)S(1)}, u32[]{:S(2)}, u32[]{:S(2)}) collective-permute-start(f32[2,128]{1,0:T(2,128)S(1)} %pad_maximum_fusion), channel_id=1, source_target_pairs={{0,8},{8,16},{16,24},{1,9},{9,17},{17,25},{2,10},{10,18},{18,26},{... | collective-permute-start | bytes 3080 | tf_op jit(solution)/shard_map/ppermute | solution.py:21
  6.1 1.6 %copy-start = (bf16[4096,256]{1,0:T(8,128)(2,1)S(1)}, bf16[4096,256]{1,0:T(8,128)(2,1)}, u32[]{:S(2)}) copy-start(bf16[4096,256]{1,0:T(8,128)(2,1)} %source_ref.1) | copy-start | bytes 6291460
  7.7 0.8 %copy-start.1 = (bf16[8,4096]{1,0:T(8,128)(2,1)S(1)}, bf16[8,4096]{1,0:T(8,128)(2,1)}, u32[]{:S(2)}) copy-start(bf16[8,4096]{1,0:T(8,128)(2,1)} %space_ref.1) | copy-start | bytes 196612
  8.5 0.7 %copy-start.2 = (bf16[16,256]{1,0:T(8,128)(2,1)S(1)}, bf16[16,256]{1,0:T(8,128)(2,1)}, u32[]{:S(2)}) copy-start(bf16[16,256]{1,0:T(8,128)(2,1)} %time_ref.1) | copy-start | bytes 24580
